TPU v7x, 32 devices: a whole 2x2x4 slice. The times are simulated.
32 devices in a mesh: sector: 4 (over y, core), row: 8 (over z, x).
Axes of the slice: x: 2, y: 2, z: 4, core: 2. Of those that a mesh axis runs over, the one named last changes fastest.
Arguments:
- amplitudes: bfloat16 [4096, 4, 8192], P('sector', None, 'row'), may hold values from -6 to 6
- next_site: bfloat16 [4, 4, 8192, 2048], P('sector', None, 'row'), may hold values from -0.03125 to 0.03125
- sector_rows: int32 [4], replicated, may hold values from 512 to 1024, as said below
- moves: int32 [2, 4], replicated, may hold values from 0 to 128, as said below
- angles: float32 [2, 4, 128], replicated, may hold values from -3.140625 to 3.140625
- ranks: int32 [4], replicated, may hold values from 256 to 1024, as said below
Outputs:
- canonical: bfloat16 [2048, 4096], P('row', 'sector')
Inputs may be any that keep to these rules, and one draw needn't show every extreme that they name: `sector_rows`: one sector has exactly 1024 live rows and another exactly 512. `moves`: the entry of the last sector is 0, every other entry is 1 or more; for each gate some pair moves exactly 128 rows. `ranks`: each sector keeps at least half of its live rows and at most all of them; one sector keeps 1024 rows and one keeps 1024 // 4.
All inputs are finite; a program needn't handle non-finite values.
Results may differ from a plain program's by a relative error of at most 0.014.
Values may be sent and summed in bfloat16 or wider, within the bound.
A program may use at most 128 MiB of HBM per device.

v0:
```python
import math

import jax
import jax.numpy as jnp
from jax import lax
from jax.sharding import PartitionSpec as P

KOUT = 2048


def shifted(x, axis, by):
    size = lax.axis_size(axis)
    pairs = [(i, i + by) for i in range(size) if 0 <= i + by < size]
    return lax.ppermute(x, axis, pairs)


def rotate_rows(
    padded, start_a, start_b, from_above, from_below, angle_here, angle_prev, count_here, count_prev
):
    slot_count = from_above.shape[0]
    slot_index = jnp.arange(slot_count)
    rows_a = lax.dynamic_slice_in_dim(padded, start_a, slot_count, 0)
    rows_b = lax.dynamic_slice_in_dim(padded, start_b, slot_count, 0)
    above_rows = from_above.astype(jnp.float32)
    below_rows = from_below.astype(jnp.float32)
    cos_here = jnp.cos(angle_here)[:, None, None]
    sin_here = jnp.sin(angle_here)[:, None, None]
    cos_prev = jnp.cos(angle_prev)[:, None, None]
    sin_prev = jnp.sin(angle_prev)[:, None, None]
    new_a = jnp.where(
        (slot_index < count_here)[:, None, None], cos_here * rows_a - sin_here * above_rows, rows_a
    )
    new_b = jnp.where(
        (slot_index < count_prev)[:, None, None], sin_prev * below_rows + cos_prev * rows_b, rows_b
    )
    padded = lax.dynamic_update_slice_in_dim(padded, new_a, start_a, 0)
    return lax.dynamic_update_slice_in_dim(padded, new_b, start_b, 0)


def per_device(amplitudes, next_site, sector_rows, moves, angles, ranks):
    sector_id = lax.axis_index("sector")
    sector_rows_count = amplitudes.shape[0]
    move_rows = sector_rows_count // 8
    row_index = jnp.arange(sector_rows_count)
    live_rows = sector_rows[sector_id]
    prev_id = jnp.maximum(sector_id - 1, 0)
    count_here = moves[:, sector_id]
    count_prev = jnp.where(sector_id > 0, moves[:, prev_id], 0)
    local_rows = jnp.where(
        (row_index < live_rows)[:, None, None], amplitudes.astype(jnp.float32), 0.0
    )
    tail_zeros = jnp.zeros((move_rows,) + local_rows.shape[1:], jnp.float32)
    padded = jnp.concatenate([local_rows, tail_zeros], 0)
    starts_a = [live_rows - count_here[0], live_rows - count_here[0] - count_here[1]]
    starts_b = [jnp.int32(0), count_prev[0]]
    for gate_index in range(2):
        send_up = lax.dynamic_slice_in_dim(padded, starts_a[gate_index], move_rows, 0).astype(
            jnp.bfloat16
        )
        send_down = lax.dynamic_slice_in_dim(padded, starts_b[gate_index], move_rows, 0).astype(
            jnp.bfloat16
        )
        from_below = shifted(send_up, "sector", 1)
        from_above = shifted(send_down, "sector", -1)
        padded = rotate_rows(
            padded,
            starts_a[gate_index],
            starts_b[gate_index],
            from_above,
            from_below,
            angles[gate_index][sector_id],
            angles[gate_index][prev_id],
            count_here[gate_index],
            count_prev[gate_index],
        )
    block_rows = padded[:sector_rows_count].astype(jnp.bfloat16)
    site_tensor = next_site[0]
    contracted = lax.psum_scatter(
        jnp.einsum("prk,lpr->kl", site_tensor, block_rows, preferred_element_type=jnp.float32),
        "row",
        scatter_dimension=0,
        tiled=True,
    ).astype(jnp.bfloat16)
    local_gram = lax.dot_general(
        contracted, contracted, (((0,), (0,)), ((), ())), preferred_element_type=jnp.float32
    )
    gram_matrix = lax.psum(local_gram, "row")
    dead_rows = (row_index >= live_rows).astype(jnp.float32)
    gram_matrix = gram_matrix + jnp.diag(dead_rows)
    factor_low = jnp.linalg.cholesky(gram_matrix)
    solved = jax.scipy.linalg.solve_triangular(
        factor_low, contracted.astype(jnp.float32).T, lower=True
    ).T
    kept_mask = ((row_index >= live_rows - ranks[sector_id]) & (row_index < live_rows)).astype(
        jnp.float32
    )
    return (solved * math.sqrt(KOUT) * kept_mask[None, :]).astype(jnp.bfloat16)


def solution(mesh):
    placed = (P("sector", None, "row"), P("sector", None, "row", None), P(), P(), P(), P())
    return jax.shard_map(
        per_device, mesh=mesh, in_specs=placed, out_specs=P("row", "sector"), check_vma=False
    )
```

profile of v0, /device:TPU:0, one launch (start us, length us, event | category | flops | bytes accessed | tf_op | source)
XLA Modules:
  0.0 804.5 jit_solution(9717891968886115581)
XLA Ops:
  10.9 12.8 %convert_select_fusion = f32[1024,4,1024]{2,0,1:T(8,128)} fusion(bf16[1024,4,1024]{2,1,0:T(4,128)(2,1)} %param.6, pred[1024]{0:T(1024)(128)(4,1)S(1)} %iota_compare_fusion.6), kind=kLoop, calls=%fused_computation.5 | loop fusion | flops 8388608 | bytes 25166848 | tf_op jit(solution)/shard_map/jit(_where)/select_n | solution.py:49
  33.5 12.4 %concatenate.30 = f32[1152,4,1024]{2,0,1:T(8,128)} pad(f32[1024,4,1024]{2,0,1:T(8,128)} %convert_select_fusion, f32[]{:T(128)} %constant.289.clone.1), padding=0_128x0_0x0_0 | pad | bytes 35651588 | tf_op jit(solution)/shard_map/concatenate | solution.py:53
  51.4 8.2 %dynamic_update_slice.12 = f32[1152,4,1024]{2,0,1:T(8,128)} dynamic-update-slice(f32[1152,4,1024]{2,0,1:T(8,128)} %concatenate.30, f32[128,4,1024]{2,0,1:T(8,128)S(1)} %subtract_select_fusion.1, s32[]{:T(128)S(6)} %select_n.62, s32[]{:T(128)} %copy.87, s32[]{:T(128)} %copy.87) | dynamic-update-slice | bytes 4194308 | tf_op jit(solution)/shard_map/dynamic_update_slice | solution.py:36
  67.6 4.3 collective-permute-start.3
  73.9 4.8 add_select_fusion
  78.8 8.4 %dynamic_update_slice.14 = f32[1152,4,1024]{2,0,1:T(8,128)} dynamic-update-slice(f32[1152,4,1024]{2,0,1:T(8,128)} %select_dynamic-update-slice_fusion, f32[128,4,1024]{2,0,1:T(8,128)} %get-tuple-element.30, s32[]{:T(128)S(6)} %select_n.67, s32[]{:T(128)} %copy.87, s32[]{:T(128)} %copy.87) | dynamic-update-slice | bytes 4194308 | tf_op jit(solution)/shard_map/dynamic_update_slice | solution.py:36
  87.2 8.1 %dynamic_update_slice.15 = f32[1152,4,1024]{2,0,1:T(8,128)} dynamic-update-slice(f32[1152,4,1024]{2,0,1:T(8,128)} %dynamic_update_slice.14, f32[128,4,1024]{2,0,1:T(8,128)S(1)} %get-tuple-element.29, s32[]{:T(128)S(6)} %select_n.68, s32[]{:T(128)} %copy.87, s32[]{:T(128)} %copy.87) | dynamic-update-slice | bytes 4194308 | tf_op jit(solution)/shard_map/dynamic_update_slice | solution.py:37
  95.3 25.0 %fusion.2 = f32[2048,1024]{0,1:T(8,128)} fusion(bf16[1,4,1024,2048]{3,2,1,0:T(8,128)(2,1)} %param.7, f32[1152,4,1024]{2,0,1:T(8,128)} %dynamic_update_slice.15), kind=kOutput, calls=%fused_computation.7 | convolution fusion | flops 17179869184 | bytes 33554432 | tf_op jit(solution)/shard_map/prk,lpr->kl/dot_general | solution.py:79
  120.4 162.9 %reduce-scatter.2.cloned.1.call-done = f32[256,1024]{0,1:T(8,128)} async-done(((f32[2048,1024]{0,1:T(8,128)}), f32[256,1024]{0,1:T(8,128)}) %reduce-scatter.2.cloned.1.call-update) | async-done | bytes 1048592 | tf_op jit(solution)/shard_map/reduce_scatter | solution.py:78
  283.3 4.4 fusion.40
  291.5 151.7 %all-reduce.4.cloned.1.call-done = f32[1024,1024]{0,1:T(8,128)} async-done(((f32[1024,1024]{0,1:T(8,128)}), f32[1024,1024]{0,1:T(8,128)}) %all-reduce.4.cloned.1.call-update) | async-done | bytes 4194320 | tf_op jit(solution)/shard_map/psum | solution.py:87
  443.2 4.8 select_add_fusion
  448.1 5.7 copy.9
  453.8 4.4 fusion.5
  460.2 11.7 %cholesky.222 = f32[128,128]{1,0:T(8,128)S(1)} custom-call(f32[128,128]{1,0:T(8,128)S(1)} %cholesky.577), custom_call_target="Cholesky" | custom-call | tf_op jit(solution)/shard_map/jit(cholesky)/cholesky | solution.py:90
  471.9 9.8 %custom-call.63 = f32[1,128,128]{1,2,0:T(8,128)S(1)} custom-call(f32[1,128,128]{2,1,0:T(8,128)S(1)} %get-tuple-element.73), custom_call_target="InvertDiagBlocksLowerTriangular" | custom-call | tf_op jit(solution)/shard_map/jit(cholesky)/cholesky | solution.py:90
  484.9 11.7 %cholesky.243 = f32[128,128]{1,0:T(8,128)S(1)} custom-call(f32[128,128]{1,0:T(8,128)S(1)} %cholesky.581), custom_call_target="Cholesky" | custom-call | tf_op jit(solution)/shard_map/jit(cholesky)/cholesky | solution.py:90
  499.7 9.8 %custom-call.64 = f32[1,128,128]{1,2,0:T(8,128)S(1)} custom-call(f32[1,128,128]{2,1,0:T(8,128)S(1)} %get-tuple-element.71), custom_call_target="InvertDiagBlocksLowerTriangular" | custom-call | tf_op jit(solution)/shard_map/jit(cholesky)/cholesky | solution.py:90
  515.0 11.7 %cholesky.466 = f32[128,128]{1,0:T(8,128)S(1)} custom-call(f32[128,128]{1,0:T(8,128)S(1)} %cholesky.586), custom_call_target="Cholesky" | custom-call | tf_op jit(solution)/shard_map/jit(cholesky)/cholesky | solution.py:90
  527.5 9.8 %custom-call.65 = f32[1,128,128]{1,2,0:T(8,128)S(1)} custom-call(f32[1,128,128]{2,1,0:T(8,128)S(1)} %get-tuple-element.69), custom_call_target="InvertDiagBlocksLowerTriangular" | custom-call | tf_op jit(solution)/shard_map/jit(cholesky)/cholesky | solution.py:90
  541.9 11.7 %cholesky.485 = f32[128,128]{1,0:T(8,128)S(1)} custom-call(f32[128,128]{1,0:T(8,128)S(1)} %cholesky.591), custom_call_target="Cholesky" | custom-call | tf_op jit(solution)/shard_map/jit(cholesky)/cholesky | solution.py:90
  554.4 9.8 %custom-call.66 = f32[1,128,128]{1,2,0:T(8,128)S(1)} custom-call(f32[1,128,128]{2,1,0:T(8,128)S(1)} %get-tuple-element.67), custom_call_target="InvertDiagBlocksLowerTriangular" | custom-call | tf_op jit(solution)/shard_map/jit(cholesky)/cholesky | solution.py:90
  568.5 12.1 %cholesky.504 = f32[128,128]{1,0:T(8,128)S(1)} custom-call(f32[128,128]{1,0:T(8,128)S(1)} %cholesky.596), custom_call_target="Cholesky" | custom-call | tf_op jit(solution)/shard_map/jit(cholesky)/cholesky | solution.py:90
  581.3 9.8 %custom-call.67 = f32[1,128,128]{1,2,0:T(8,128)S(1)} custom-call(f32[1,128,128]{2,1,0:T(8,128)S(1)} %get-tuple-element.65), custom_call_target="InvertDiagBlocksLowerTriangular" | custom-call | tf_op jit(solution)/shard_map/jit(cholesky)/cholesky | solution.py:90
  595.4 11.7 %cholesky.524 = f32[128,128]{1,0:T(8,128)S(1)} custom-call(f32[128,128]{1,0:T(8,128)S(1)} %cholesky.601), custom_call_target="Cholesky" | custom-call | tf_op jit(solution)/shard_map/jit(cholesky)/cholesky | solution.py:90
  607.8 9.8 %custom-call.68 = f32[1,128,128]{1,2,0:T(8,128)S(1)} custom-call(f32[1,128,128]{2,1,0:T(8,128)S(1)} %get-tuple-element.63), custom_call_target="InvertDiagBlocksLowerTriangular" | custom-call | tf_op jit(solution)/shard_map/jit(cholesky)/cholesky | solution.py:90
  621.5 11.7 %cholesky.544 = f32[128,128]{1,0:T(8,128)S(1)} custom-call(f32[128,128]{1,0:T(8,128)S(1)} %cholesky.606), custom_call_target="Cholesky" | custom-call | tf_op jit(solution)/shard_map/jit(cholesky)/cholesky | solution.py:90
  634.0 9.8 %custom-call.69 = f32[1,128,128]{1,2,0:T(8,128)S(1)} custom-call(f32[1,128,128]{2,1,0:T(8,128)S(1)} %get-tuple-element.61), custom_call_target="InvertDiagBlocksLowerTriangular" | custom-call | tf_op jit(solution)/shard_map/jit(cholesky)/cholesky | solution.py:90
  646.8 11.7 %cholesky.562 = f32[128,128]{1,0:T(8,128)S(1)} custom-call(f32[128,128]{1,0:T(8,128)S(1)} %convolution_subtract_fusion.13), custom_call_target="Cholesky" | custom-call | tf_op jit(solution)/shard_map/jit(cholesky)/cholesky | solution.py:90
  669.6 4.8 select_select_fusion
  674.5 28.6 %while.1 = (s32[]{:T(128)}, f32[1024,1024]{0,1:T(8,128)}, s32[8,2]{0,1:T(2,128)S(1)}, f32[8,128,128]{2,1,0:T(8,128)}, s32[]{:T(128)}) while((s32[]{:T(128)}, f32[1024,1024]{0,1:T(8,128)}, s32[8,2]{0,1:T(2,128)S(1)}, f32[8,128,128]{2,1,0:T(8,128)}, s32[]{:T(128)}) %tuple.65), condition=%wide.while_cond, body=%wide.while_body.sunk | while | flops 2 | bytes 393829 | solution.py:91
  703.1 79.6 %custom-call.70 = f32[8,128,128]{1,2,0:T(8,128)S(1)} custom-call(f32[8,128,128]{2,1,0:T(8,128)} %get-tuple-element.12), custom_call_target="InvertDiagBlocksLowerTriangular" | custom-call | tf_op jit(solution)/shard_map/jit(_solve_triangular)/triangular_solve | solution.py:91
  (155 shorter events, 115.0 us)
Async XLA Ops:
  6.5 276.7 %reduce-scatter.2.cloned.1.call-start = ((), (), s32[]{:S(2)}) async-start(), calls=%async_computation.1 | async-start | bytes 9437184 | tf_op jit(solution)/shard_map/reduce_scatter | solution.py:78
  26.3 21.6 %collective-permute-start = (bf16[128,4,1024]{2,0,1:T(8,128)(2,1)S(1)}, bf16[128,4,1024]{2,0,1:T(8,128)(2,1)S(1)}, u32[]{:S(2)}, u32[]{:S(2)}) collective-permute-start(bf16[128,4,1024]{2,0,1:T(8,128)(2,1)S(1)} %get-tuple-element.34), channel_id=1, source_target_pairs={{8,0},{16,8},{24,16},{9,1},{17,9},{25,17},{10,2},{18,10},{26,18},{... | collective-permute-start | bytes 3145736 | tf_op jit(solution)/shard_map/ppermute | solution.py:14
  27.6 32.0 %collective-permute-start.1 = (bf16[128,4,1024]{2,0,1:T(8,128)(2,1)S(1)}, bf16[128,4,1024]{2,0,1:T(8,128)(2,1)}, u32[]{:S(2)}, u32[]{:S(2)}) collective-permute-start(bf16[128,4,1024]{2,0,1:T(8,128)(2,1)S(1)} %get-tuple-element.33), channel_id=1, source_target_pairs={{0,8},{8,16},{16,24},{1,9},{9,17},{17,25},{2,10},{10,18},{18,26},{... | collective-permute-start | bytes 3145736 | tf_op jit(solution)/shard_map/ppermute | solution.py:14
  33.5 14.3 %copy-start.3 = (f32[2,4,128]{2,1,0:T(4,128)S(1)}, f32[2,4,128]{2,1,0:T(4,128)}, u32[]{:S(2)}) copy-start(f32[2,4,128]{2,1,0:T(4,128)} %param.10) | copy-start | bytes 12292
  47.8 1.0 copy-start.2
  66.3 7.0 collective-permute-start.2
  67.6 6.3 collective-permute-start.3
  120.3 322.9 %all-reduce.4.cloned.1.call-start = ((), (), s32[]{:S(2)}) async-start(), calls=%async_computation.2 | async-start | bytes 8388608 | tf_op jit(solution)/shard_map/psum | solution.py:87
  287.7 0.7 copy-start.4
  287.7 3.6 copy-start.1
  458.2 1.9 copy-start
Sparse Core Ops, SparseCore 0:
  120.4 162.7 reduce-scatter.1
  287.9 155.3 all-reduce.3
where the time goes:
time: 812 us; the launch traced here: 804 us
  waiting for transfers between devices  315 us (39%)
  other arithmetic  291 us (36%)
  local copies, waits for them, and re-layouts  92.9 us (11%)
  matrix products  69.8 us (9%)
  between operations  24.1 us (3%)
  starting transfers between devices  11 us (1%)
    another operation x31, other arithmetic, per_device(): factor_low = jnp.linalg.cholesky(gram_matrix)  168 us
    reduce_scatter x1, waiting for transfers between devices, per_device(): lax.psum_scatter(jnp.einsum('prk,lpr->kl', site_tensor, block_rows, prefe...  163 us
    psum x1, waiting for transfers between devices, per_device(): gram_matrix = lax.psum(local_gram, 'row')  152 us
    another operation x3, other arithmetic, per_device(): jax.scipy.linalg.solve_triangular(factor_low, contracted.astype(jnp.float...  84.4 us
    another operation x40, local copies, waits for them, and re-layouts  28.5 us
    another operation x14, matrix products, per_device(): factor_low = jnp.linalg.cholesky(gram_matrix)  27 us
    dot_general x1, matrix products, per_device(): jnp.einsum('prk,lpr->kl', site_tensor, block_rows, preferred_element_type...  25 us
    dynamic_update_slice x2, local copies, waits for them, and re-layouts, rotate_rows(): padded = lax.dynamic_update_slice_in_dim(padded, new_a, start_a, 0)  16.6 us
  transfers between devices with their start and end apart: 6, of which 3 were waited for; matrix products, arithmetic and copies ran while one was open for 3% of the time, Pallas kernels for 0%

commit v1 on v0

v1 whole, which is shorter than its diff:
```python
import math

import jax
import jax.numpy as jnp
from jax import lax
from jax.experimental import pallas as pl
from jax.experimental.pallas import tpu as pltpu
from jax.sharding import PartitionSpec as P

KOUT = 2048


def shifted(x, axis, by):
    size = lax.axis_size(axis)
    pairs = [(i, i + by) for i in range(size) if 0 <= i + by < size]
    return lax.ppermute(x, axis, pairs)


TILE = 128
GROUP = 4


def rotate_rows(padded, start, here, other, angle, count, sign):
    slot_index = jnp.arange(here.shape[0])
    mine = here.astype(jnp.float32)
    cos = jnp.cos(angle)[:, None, None]
    sin = sign * jnp.sin(angle)[:, None, None]
    rotated = (cos * mine + sin * other.astype(jnp.float32)).astype(jnp.bfloat16)
    rows = lax.dynamic_slice_in_dim(padded, start, here.shape[0], 0)
    rows = jnp.where((slot_index < count)[:, None, None], rotated, rows)
    return lax.dynamic_update_slice_in_dim(padded, rows, start, 0)


def inverse_factor(tile):
    slabs = TILE // 8
    lane = lax.broadcasted_iota(jnp.int32, (8, TILE), 1)
    sub = lax.broadcasted_iota(jnp.int32, (8, TILE), 0)
    a = [tile[8 * i : 8 * i + 8] for i in range(slabs)]
    for first in range(0, TILE, GROUP):
        top = first // 8
        cols = [
            {i: jnp.broadcast_to(a[i][:, first + q : first + q + 1], (8, TILE)) for i in range(top, slabs)}
            for q in range(GROUP)
        ]
        for q in range(GROUP):
            j = first + q
            r = j - 8 * top
            inv = 1.0 / cols[q][top][r : r + 1]
            row = a[top][r : r + 1]
            heads = {p: cols[p][top][r : r + 1] for p in range(q + 1, GROUP)}
            for i in range(top, slabs):
                m = cols[q][i] * inv
                hit = lane == j
                if i == top:
                    m = jnp.where(sub > r, m, 0.0)
                    hit = hit & (sub > r)
                for p in range(q + 1, GROUP):
                    cols[p][i] = cols[p][i] - m * heads[p]
                a[i] = jnp.where(hit, -m, a[i] - m * row)
    out = []
    for i in range(slabs):
        on = lane == sub + 8 * i
        pivot = jnp.sum(jnp.where(on, a[i], 0.0), axis=1, keepdims=True)
        unit = jnp.where(lane < sub + 8 * i, a[i], jnp.where(on, 1.0, 0.0))
        out.append(unit * lax.rsqrt(pivot))
    return jnp.concatenate(out, 0)


def dot_full(x, y, dims):
    return lax.dot_general(
        x, y, (dims, ((), ())), precision=lax.Precision.HIGHEST, preferred_element_type=jnp.float32
    )


def whiten_kernel(gram_ref, cols_ref, scale_ref, out_ref, work, rest, panel):
    size = work.shape[0]
    blocks = size // TILE
    work[...] = gram_ref[...]
    rest[...] = cols_ref[...].astype(jnp.float32)

    def block_step(k, carry):
        at = pl.ds(pl.multiple_of(k * TILE, TILE), TILE)
        inverse = inverse_factor(work[at, at])
        solved = dot_full(rest[:, at], inverse, ((1,), (1,)))
        out_ref[:, at] = (solved * scale_ref[:, at]).astype(jnp.bfloat16)
        panel[...] = dot_full(inverse, work[at, :], ((1,), (0,)))

        def trail(i, inner):
            to = pl.ds(pl.multiple_of(i * TILE, TILE), TILE)
            part = panel[:, to]
            work[to, :] = work[to, :] - dot_full(part.T, panel[...], ((1,), (0,)))
            rest[:, to] = rest[:, to] - dot_full(solved, part, ((1,), (0,)))
            return inner

        return lax.fori_loop(k + 1, blocks, trail, carry)

    lax.fori_loop(0, blocks, block_step, 0)


def whiten(gram_matrix, contracted, scale):
    rows, size = contracted.shape
    vmem = pl.BlockSpec(memory_space=pltpu.VMEM)
    return pl.pallas_call(
        whiten_kernel,
        out_shape=jax.ShapeDtypeStruct((rows, size), jnp.bfloat16),
        in_specs=[vmem] * 3,
        out_specs=vmem,
        scratch_shapes=[
            pltpu.VMEM((size, size), jnp.float32),
            pltpu.VMEM((rows, size), jnp.float32),
            pltpu.VMEM((TILE, size), jnp.float32),
        ],
        compiler_params=pltpu.CompilerParams(vmem_limit_bytes=40 * 1024 * 1024),
    )(gram_matrix, contracted, scale)


def per_device(amplitudes, next_site, sector_rows, moves, angles, ranks):
    sector_id = lax.axis_index("sector")
    sector_rows_count = amplitudes.shape[0]
    move_rows = sector_rows_count // 8
    row_index = jnp.arange(sector_rows_count)
    live_rows = sector_rows[sector_id]
    prev_id = jnp.maximum(sector_id - 1, 0)
    count_here = moves[:, sector_id]
    count_prev = jnp.where(sector_id > 0, moves[:, prev_id], 0)
    local_rows = jnp.where((row_index < live_rows)[:, None, None], amplitudes, jnp.bfloat16(0))
    padded = jnp.pad(local_rows, ((0, move_rows), (0, 0), (0, 0)))
    starts_a = [live_rows - count_here[0], live_rows - count_here[0] - count_here[1]]
    starts_b = [jnp.int32(0), count_prev[0]]
    ends_a = [lax.dynamic_slice_in_dim(padded, at, move_rows, 0) for at in starts_a]
    ends_b = [lax.dynamic_slice_in_dim(padded, at, move_rows, 0) for at in starts_b]
    from_below = shifted(jnp.concatenate(ends_a, 0), "sector", 1)
    from_above = shifted(jnp.concatenate(ends_b, 0), "sector", -1)
    for gate in range(2):
        part = slice(gate * move_rows, (gate + 1) * move_rows)
        padded = rotate_rows(
            padded, starts_a[gate], ends_a[gate], from_above[part],
            angles[gate][sector_id], count_here[gate], -1.0,
        )
        padded = rotate_rows(
            padded, starts_b[gate], ends_b[gate], from_below[part],
            angles[gate][prev_id], count_prev[gate], 1.0,
        )
    block_rows = padded[:sector_rows_count]
    partial = jnp.einsum(
        "prk,lpr->kl", next_site[0], block_rows, preferred_element_type=jnp.float32
    ).astype(jnp.bfloat16)
    contracted = lax.psum_scatter(partial, "row", scatter_dimension=0, tiled=True)
    gathered = lax.all_gather(contracted, "row", axis=0, tiled=True)
    gram_matrix = lax.dot_general(
        gathered, gathered, (((0,), (0,)), ((), ())), preferred_element_type=jnp.float32
    )
    gram_matrix = gram_matrix + jnp.diag((row_index >= live_rows).astype(jnp.float32))
    kept = (row_index >= live_rows - ranks[sector_id]) & (row_index < live_rows)
    scale = jnp.where(kept, jnp.float32(math.sqrt(KOUT)), 0.0)[None, :]
    return whiten(gram_matrix, contracted, scale)


def solution(mesh):
    placed = (P("sector", None, "row"), P("sector", None, "row", None), P(), P(), P(), P())
    return jax.shard_map(
        per_device, mesh=mesh, in_specs=placed, out_specs=P("row", "sector"), check_vma=False
    )
```

time: 812 us -> 391 us (0.48)
  other arithmetic: 291 us -> 31.5 us
  waiting for transfers between devices: 315 us -> 170 us
  Pallas kernels: 0 us -> 76.3 us
  local copies, waits for them, and re-layouts: 92.9 us -> 35.9 us
  matrix products: 69.8 us -> 31.5 us
  starting transfers between devices: 11 us -> 26.4 us
    another operation x34 -> x0, other arithmetic: 253 us -> none  [the longest x31 168 us: per_device(): factor_low = jnp.linalg.cholesky(gram_matrix)]
    psum x1 -> x0, waiting for transfers between devices: 152 us -> none  [per_device(): gram_matrix = lax.psum(local_gram, 'row')]
    pallas_call x0 -> x1, Pallas kernels: none -> 76.3 us  [whiten(): pl.pallas_call(whiten_kernel, out_shape=jax.ShapeDtypeStruct((rows, size)...]
    all_gather x0 -> x1, waiting for transfers between devices: none -> 72.3 us  [per_device(): gathered = lax.all_gather(contracted, 'row', axis=0, tiled=True)]
    reduce_scatter x1, waiting for transfers between devices: 163 us -> 95.1 us  [per_device(): lax.psum_scatter(partial, 'row', scatter_dimension=0, tiled=True)]
    another operation x29 -> x0, matrix products: 40.4 us -> none  [the longest x14 27 us: per_device(): factor_low = jnp.linalg.cholesky(gram_matrix)]
    another operation x66 -> x0, local copies, waits for them, and re-layouts: 37.4 us -> none
    ppermute x4 -> x2, starting transfers between devices: 10.9 us -> 26.1 us  [shifted(): return lax.ppermute(x, axis, pairs)]
  transfers between devices with their start and end apart: 6 -> 4, of which waited for: 3 -> 3; matrix products, arithmetic and copies ran while one was open for 3% -> 5% of each run, Pallas kernels for 0% -> 0%
where the time goes in v1:
time: 391 us; the launch traced here: 390 us
  waiting for transfers between devices  170 us (43%)
  Pallas kernels  76.3 us (20%)
  local copies, waits for them, and re-layouts  35.9 us (9%)
  other arithmetic  31.5 us (8%)
  matrix products  31.5 us (8%)
  starting transfers between devices  26.4 us (7%)
  between operations  18.4 us (5%)
    reduce_scatter x1, waiting for transfers between devices, per_device(): lax.psum_scatter(partial, 'row', scatter_dimension=0, tiled=True)  95.1 us
    pallas_call x1, Pallas kernels, whiten(): pl.pallas_call(whiten_kernel, out_shape=jax.ShapeDtypeStruct((rows, size)...  76.3 us
    all_gather x1, waiting for transfers between devices, per_device(): gathered = lax.all_gather(contracted, 'row', axis=0, tiled=True)  72.3 us
    ppermute x2, starting transfers between devices, shifted(): return lax.ppermute(x, axis, pairs)  26.1 us
    dot_general x1, matrix products, per_device(): jnp.einsum('prk,lpr->kl', next_site[0], block_rows, preferred_element_typ...  23.9 us
    dynamic_update_slice x3, local copies, waits for them, and re-layouts, rotate_rows(): return lax.dynamic_update_slice_in_dim(padded, rows, start, 0)  23.4 us
    select_n x1, other arithmetic, per_device(): jnp.where((row_index < live_rows)[:, None, None], amplitudes, jnp.bfloat1...  12.2 us
    select_n x3, other arithmetic, rotate_rows(): rows = jnp.where((slot_index < count)[:, None, None], rotated, rows)  8.79 us
  transfers between devices with their start and end apart: 4, of which 3 were waited for; matrix products, arithmetic and copies ran while one was open for 5% of the time, Pallas kernels for 0%

profile of v1, /device:TPU:0, one launch (start us, length us, event | category | flops | bytes accessed | tf_op | source)
XLA Modules:
  0.0 389.6 jit_solution(4986717570446346334)
XLA Ops:
  6.5 0.8 constant_dynamic-slice_fusion.8
  7.4 0.6 fusion.21
  9.1 1.2 dynamic_slice.46
  10.3 0.6 iota_compare_fusion.2
  11.5 12.2 %copy_select_fusion = bf16[1024,4,1024]{2,0,1:T(8,128)(2,1)} fusion(bf16[1024,4,1024]{2,1,0:T(4,128)(2,1)} %param.6, pred[1024]{0:T(1024)(128)(4,1)S(1)} %iota_compare_fusion.2), kind=kLoop, calls=%fused_computation.4 | loop fusion | flops 4194304 | bytes 16778240 | tf_op jit(solution)/shard_map/jit(_where)/select_n | solution.py:126
  23.7 2.0 fusion.19
  25.7 0.2 pad_maximum_fusion
  25.9 1.3 collective-permute-start
  29.1 0.7 iota_compare_fusion.6
  29.9 2.1 collective-permute-done
  32.1 3.1 fusion.12
  35.2 1.5 pad_maximum_fusion.1
  36.7 24.8 %collective-permute-start.1 = (bf16[256,4,1024]{2,0,1:T(8,128)(2,1)}, bf16[256,4,1024]{2,0,1:T(8,128)(2,1)S(1)}, u32[]{:S(2)}, u32[]{:S(2)}) collective-permute-start(bf16[256,4,1024]{2,0,1:T(8,128)(2,1)} %pad_maximum_fusion.1), channel_id=1, source_target_pairs={{0,8},{8,16},{16,24},{1,9},{9,17},{17,25},{2,10},{10,18},{18,26},{... | collective-permute-start | bytes 6291464 | tf_op jit(solution)/shard_map/ppermute | solution.py:16
  61.5 8.1 %pad.4 = bf16[1152,4,1024]{2,0,1:T(8,128)(2,1)} pad(bf16[1024,4,1024]{2,0,1:T(8,128)(2,1)} %copy_select_fusion, bf16[]{:T(256)} %constant.24.clone.1), padding=0_128x0_0x0_0 | pad | bytes 17825794 | tf_op jit(solution)/shard_map/jit(_pad)/pad | solution.py:127
  69.6 0.5 iota_compare_fusion.5
  70.2 0.6 iota_compare_fusion.4
  70.8 0.7 iota_compare_fusion.3
  71.5 7.8 %dynamic_update_slice.12 = bf16[1152,4,1024]{2,0,1:T(8,128)(2,1)} dynamic-update-slice(bf16[1152,4,1024]{2,0,1:T(8,128)(2,1)} %pad.4, bf16[128,4,1024]{2,0,1:T(8,128)(2,1)S(1)} %get-tuple-element.5, s32[]{:T(128)S(6)} %select_n.69, s32[]{:T(128)} %constant.22.clone.1, s32[]{:T(128)} %constant.22.clone.1) | dynamic-update-slice | bytes 2097156 | tf_op jit(solution)/shard_map/dynamic_update_slice | solution.py:31
  79.4 3.4 fusion.14
  82.7 3.0 fusion.15
  85.7 7.8 %dynamic_update_slice.14 = bf16[1152,4,1024]{2,0,1:T(8,128)(2,1)} dynamic-update-slice(bf16[1152,4,1024]{2,0,1:T(8,128)(2,1)} %fusion.14, bf16[128,4,1024]{2,0,1:T(8,128)(2,1)S(1)} %fusion.15, s32[]{:T(128)S(6)} %select_n.74, s32[]{:T(128)} %constant.22.clone.1, s32[]{:T(128)} %constant.22.clone.1) | dynamic-update-slice | bytes 2097156 | tf_op jit(solution)/shard_map/dynamic_update_slice | solution.py:31
  93.6 2.7 fusion.16
  96.3 7.8 %dynamic_update_slice.15 = bf16[1152,4,1024]{2,0,1:T(8,128)(2,1)} dynamic-update-slice(bf16[1152,4,1024]{2,0,1:T(8,128)(2,1)} %dynamic_update_slice.14, bf16[128,4,1024]{2,0,1:T(8,128)(2,1)S(1)} %fusion.16, s32[]{:T(128)S(6)} %select_n.72, s32[]{:T(128)} %constant.22.clone.1, s32[]{:T(128)} %constant.22.clone.1) | dynamic-update-slice | bytes 2097156 | tf_op jit(solution)/shard_map/dynamic_update_slice | solution.py:31
  104.0 23.9 %fusion.7 = bf16[2048,1024]{1,0:T(8,128)(2,1)} fusion(bf16[1,4,1024,2048]{3,2,1,0:T(8,128)(2,1)} %param.7, bf16[1152,4,1024]{2,0,1:T(8,128)(2,1)} %dynamic_update_slice.15), kind=kOutput, calls=%fused_computation.7 | convolution fusion | flops 17181966336 | bytes 29360128 | tf_op jit(solution)/shard_map/prk,lpr->kl/dot_general | solution.py:145
  128.0 0.3 all-gather.2.cloned.1.call-start
  128.2 95.1 %reduce-scatter.2.cloned.1.call-done.cols_ref = bf16[256,1024]{1,0:T(8,128)(2,1)} async-done(((bf16[2048,1024]{1,0:T(8,128)(2,1)}), bf16[256,1024]{1,0:T(8,128)(2,1)}) %reduce-scatter.2.cloned.1.call-update) | async-done | bytes 524304 | tf_op jit(solution)/shard_map/reduce_scatter | solution.py:148
  223.3 0.6 dynamic_slice.60
  225.2 0.7 fusion.17
  225.8 0.7 and_select_fusion.scale_ref
  226.5 72.3 %all-gather.2.cloned.1.call-done = bf16[2048,1024]{1,0:T(8,128)(2,1)} async-done(((bf16[256,1024]{1,0:T(8,128)(2,1)}), bf16[2048,1024]{1,0:T(8,128)(2,1)}) %all-gather.2.cloned.1.call-update) | async-done | bytes 4194320 | tf_op jit(solution)/shard_map/all_gather | solution.py:149
  298.8 7.6 %select_add_fusion.gram_ref = f32[1024,1024]{1,0:T(8,128)S(1)} fusion(f32[1024]{0:T(1024)S(1)} %fusion.17, bf16[2048,1024]{1,0:T(8,128)(2,1)} %all-gather.2.cloned.1.call-done), kind=kOutput, calls=%fused_computation.5 | convolution fusion | flops 4298113024 | bytes 8392704 | tf_op jit(solution)/shard_map/dot_general | solution.py:150
  306.4 76.3 %shard_map.64 = bf16[256,1024]{1,0:T(8,128)(2,1)} custom-call(f32[1024,1024]{1,0:T(8,128)S(1)} %select_add_fusion.gram_ref, bf16[256,1024]{1,0:T(8,128)(2,1)S(1)} %copy-done, f32[1,1024]{1,0:T(1,128)S(1)} %and_select_fusion.scale_ref), custom_call_target="tpu_custom_call" | custom-call | tf_op jit(solution)/shard_map/pallas_call | solution.py:103
  (13 shorter events, 0.2 us)
Async XLA Ops:
  6.5 216.8 %reduce-scatter.2.cloned.1.call-start = ((), (), s32[]{:S(2)}) async-start(), calls=%async_computation.1 | async-start | bytes 4718592 | tf_op jit(solution)/shard_map/reduce_scatter | solution.py:148
  25.7 4.2 %copy-start.1 = (f32[2,4,128]{2,1,0:T(4,128)S(1)}, f32[2,4,128]{2,1,0:T(4,128)}, u32[]{:S(2)}) copy-start(f32[2,4,128]{2,1,0:T(4,128)} %param.10) | copy-start | bytes 12292
  25.9 6.2 %collective-permute-start = (bf16[256,4,1024]{2,0,1:T(8,128)(2,1)S(1)}, bf16[256,4,1024]{2,0,1:T(8,128)(2,1)}, u32[]{:S(2)}, u32[]{:S(2)}) collective-permute-start(bf16[256,4,1024]{2,0,1:T(8,128)(2,1)S(1)} %pad_maximum_fusion), channel_id=1, source_target_pairs={{8,0},{16,8},{24,16},{9,1},{17,9},{25,17},{10,2},{18,10},{26,18},{... | collective-permute-start | bytes 6291464 | tf_op jit(solution)/shard_map/ppermute | solution.py:16
  36.7 42.7 %collective-permute-start.1 = (bf16[256,4,1024]{2,0,1:T(8,128)(2,1)}, bf16[256,4,1024]{2,0,1:T(8,128)(2,1)S(1)}, u32[]{:S(2)}, u32[]{:S(2)}) collective-permute-start(bf16[256,4,1024]{2,0,1:T(8,128)(2,1)} %pad_maximum_fusion.1), channel_id=1, source_target_pairs={{0,8},{8,16},{16,24},{1,9},{9,17},{17,25},{2,10},{10,18},{18,26},{... | collective-permute-start | bytes 6291464 | tf_op jit(solution)/shard_map/ppermute | solution.py:16
  127.9 95.4 %copy-start.2 = (s32[4]{0:T(128)S(1)}, s32[4]{0:T(128)}, u32[]{:S(2)}) copy-start(s32[4]{0:T(128)} %param.11) | copy-start | bytes 52
  128.0 170.9 %all-gather.2.cloned.1.call-start = ((), (), s32[]{:S(2)}) async-start(), calls=%async_computation.2 | async-start | bytes 4718592 | tf_op jit(solution)/shard_map/all_gather | solution.py:149
  226.5 79.9 %copy-start = (bf16[256,1024]{1,0:T(8,128)(2,1)S(1)}, bf16[256,1024]{1,0:T(8,128)(2,1)}, u32[]{:S(2)}) copy-start(bf16[256,1024]{1,0:T(8,128)(2,1)} %reduce-scatter.2.cloned.1.call-done.cols_ref) | copy-start | bytes 1572868
Sparse Core Ops, SparseCore 0:
  128.1 95.1 reduce-scatter.1
  225.6 73.1 all-gather.1

commit v2 on v1

--- a/solution.py
+++ b/solution.py
@@ -26,8 +26,7 @@
     cos = jnp.cos(angle)[:, None, None]
     sin = sign * jnp.sin(angle)[:, None, None]
     rotated = (cos * mine + sin * other.astype(jnp.float32)).astype(jnp.bfloat16)
-    rows = lax.dynamic_slice_in_dim(padded, start, here.shape[0], 0)
-    rows = jnp.where((slot_index < count)[:, None, None], rotated, rows)
+    rows = jnp.where((slot_index < count)[:, None, None], rotated, here)
     return lax.dynamic_update_slice_in_dim(padded, rows, start, 0)
 
 
@@ -123,20 +122,23 @@
     prev_id = jnp.maximum(sector_id - 1, 0)
     count_here = moves[:, sector_id]
     count_prev = jnp.where(sector_id > 0, moves[:, prev_id], 0)
-    local_rows = jnp.where((row_index < live_rows)[:, None, None], amplitudes, jnp.bfloat16(0))
-    padded = jnp.pad(local_rows, ((0, move_rows), (0, 0), (0, 0)))
+    wide_rows = jnp.pad(amplitudes, ((0, move_rows), (0, 0), (0, 0)))
+    wide_index = jnp.arange(sector_rows_count + move_rows)
+    padded = jnp.where((wide_index < live_rows)[:, None, None], wide_rows, jnp.bfloat16(0))
     starts_a = [live_rows - count_here[0], live_rows - count_here[0] - count_here[1]]
     starts_b = [jnp.int32(0), count_prev[0]]
     ends_a = [lax.dynamic_slice_in_dim(padded, at, move_rows, 0) for at in starts_a]
     ends_b = [lax.dynamic_slice_in_dim(padded, at, move_rows, 0) for at in starts_b]
     from_below = shifted(jnp.concatenate(ends_a, 0), "sector", 1)
     from_above = shifted(jnp.concatenate(ends_b, 0), "sector", -1)
-    for gate in range(2):
+    for gate in (1, 0):
         part = slice(gate * move_rows, (gate + 1) * move_rows)
         padded = rotate_rows(
             padded, starts_a[gate], ends_a[gate], from_above[part],
             angles[gate][sector_id], count_here[gate], -1.0,
         )
+    for gate in (0, 1):
+        part = slice(gate * move_rows, (gate + 1) * move_rows)
         padded = rotate_rows(
             padded, starts_b[gate], ends_b[gate], from_below[part],
             angles[gate][prev_id], count_prev[gate], 1.0,

time: 391 us -> 407 us (1.041)
  waiting for transfers between devices: 170 us -> 199 us
  starting transfers between devices: 26.4 us -> 5.41 us
  local copies, waits for them, and re-layouts: 35.9 us -> 46.7 us
    ppermute x2, starting transfers between devices: 26.1 us -> 5.14 us  [shifted(): return lax.ppermute(x, axis, pairs)]
    unnamed x6 -> x10, local copies, waits for them, and re-layouts: 0.01 us -> 18 us
    reduce_scatter x1, waiting for transfers between devices: 95.1 us -> 110 us  [per_device(): lax.psum_scatter(partial, 'row', scatter_dimension=0, tiled=True)]
    ppermute x2, waiting for transfers between devices: 2.13 us -> 16.2 us  [shifted(): return lax.ppermute(x, axis, pairs)]
    pad x1 -> x0, local copies, waits for them, and re-layouts: 8.07 us -> none  [per_device(): padded = jnp.pad(local_rows, ((0, move_rows), (0, 0), (0, 0)))]
  transfers between devices with their start and end apart: 4 -> 4, of which waited for: 3 -> 4; matrix products, arithmetic and copies ran while one was open for 5% -> 3% of each run, Pallas kernels for 0% -> 0%
where the time goes in v2:
time: 407 us; the launch traced here: 406 us
  waiting for transfers between devices  199 us (49%)
  Pallas kernels  76.3 us (19%)
  local copies, waits for them, and re-layouts  46.7 us (11%)
  matrix products  31.5 us (8%)
  other arithmetic  28.9 us (7%)
  between operations  18.4 us (5%)
  starting transfers between devices  5.41 us (1%)
    reduce_scatter x1, waiting for transfers between devices, per_device(): lax.psum_scatter(partial, 'row', scatter_dimension=0, tiled=True)  110 us
    pallas_call x1, Pallas kernels, whiten(): pl.pallas_call(whiten_kernel, out_shape=jax.ShapeDtypeStruct((rows, size)...  76.3 us
    all_gather x1, waiting for transfers between devices, per_device(): gathered = lax.all_gather(contracted, 'row', axis=0, tiled=True)  72.4 us
    dot_general x1, matrix products, per_device(): jnp.einsum('prk,lpr->kl', next_site[0], block_rows, preferred_element_typ...  23.9 us
    dynamic_update_slice x3, local copies, waits for them, and re-layouts, rotate_rows(): return lax.dynamic_update_slice_in_dim(padded, rows, start, 0)  23.7 us
    unnamed x10, local copies, waits for them, and re-layouts  18 us
    ppermute x2, waiting for transfers between devices, shifted(): return lax.ppermute(x, axis, pairs)  16.2 us
    select_n x1, other arithmetic, per_device(): jnp.where((wide_index < live_rows)[:, None, None], wide_rows, jnp.bfloat1...  10.2 us
  transfers between devices with their start and end apart: 4, of which 4 were waited for; matrix products, arithmetic and copies ran while one was open for 3% of the time, Pallas kernels for 0%

profile of v2, /device:TPU:0, one launch (start us, length us, event | category | flops | bytes accessed | tf_op | source)
XLA Modules:
  0.0 406.1 jit_solution(12218058557019634268)
XLA Ops:
  6.5 1.2 dynamic_slice.36
  7.8 0.8 fusion.18
  8.6 0.5 fusion.21
  10.9 0.7 iota_compare_fusion.1
  11.6 9.5 %copy.7 = bf16[1024,4,1024]{2,0,1:T(8,128)(2,1)} copy(bf16[1024,4,1024]{2,1,0:T(4,128)(2,1)} %param.6) | data formatting | bytes 16777216 | tf_op args[0]
  21.1 10.2 %pad_select_fusion = bf16[1152,4,1024]{2,0,1:T(8,128)(2,1)} fusion(bf16[1024,4,1024]{2,0,1:T(8,128)(2,1)} %copy.7, pred[1152]{0:T(1024)(128)(4,1)S(1)} %iota_compare_fusion.1), kind=kLoop, calls=%fused_computation.2 | loop fusion | flops 4718592 | bytes 17826944 | tf_op jit(solution)/shard_map/jit(_where)/select_n | solution.py:127
  31.3 2.7 fusion.19
  34.0 1.5 pad_maximum_fusion.1
  35.5 3.7 collective-permute-start.1
  41.1 0.6 iota_compare_fusion.3
  42.0 3.4 fusion.15
  45.3 1.6 pad_maximum_fusion
  47.0 1.5 collective-permute-start
  48.4 8.5 %copy.11 = bf16[1152,4,1024]{2,0,1:T(8,128)(2,1)} copy(bf16[1152,4,1024]{2,0,1:T(8,128)(2,1)} %pad_select_fusion) | data formatting | bytes 18874368
  56.9 0.6 iota_compare_fusion.5
  57.4 0.6 iota_compare_fusion.6
  58.0 0.6 iota_compare_fusion.4
  58.7 16.0 %collective-permute-done = bf16[256,4,1024]{2,0,1:T(8,128)(2,1)} collective-permute-done((bf16[256,4,1024]{2,0,1:T(8,128)(2,1)}, bf16[256,4,1024]{2,0,1:T(8,128)(2,1)}, u32[]{:S(2)}, u32[]{:S(2)}) %collective-permute-start) | collective-permute-done | bytes 2097184 | tf_op jit(solution)/shard_map/ppermute | solution.py:16
  74.7 3.8 fusion.13
  78.5 8.1 %dynamic_update_slice.12 = bf16[1152,4,1024]{2,0,1:T(8,128)(2,1)} dynamic-update-slice(bf16[1152,4,1024]{2,0,1:T(8,128)(2,1)} %copy.11, bf16[128,4,1024]{2,0,1:T(8,128)(2,1)} %get-tuple-element.11, s32[]{:T(128)S(6)} %select_n.66, s32[]{:T(128)} %constant.22.clone.1, s32[]{:T(128)} %constant.22.clone.1) | dynamic-update-slice | bytes 2097156 | tf_op jit(solution)/shard_map/dynamic_update_slice | solution.py:30
  86.7 7.7 %dynamic_update_slice.13 = bf16[1152,4,1024]{2,0,1:T(8,128)(2,1)} dynamic-update-slice(bf16[1152,4,1024]{2,0,1:T(8,128)(2,1)} %dynamic_update_slice.12, bf16[128,4,1024]{2,0,1:T(8,128)(2,1)S(1)} %get-tuple-element.10, s32[]{:T(128)S(6)} %select_n.71, s32[]{:T(128)} %constant.22.clone.1, s32[]{:T(128)} %constant.22.clone.1) | dynamic-update-slice | bytes 2097156 | tf_op jit(solution)/shard_map/dynamic_update_slice | solution.py:30
  94.4 3.2 fusion.16
  97.6 7.8 %dynamic_update_slice.15 = bf16[1152,4,1024]{2,0,1:T(8,128)(2,1)} dynamic-update-slice(bf16[1152,4,1024]{2,0,1:T(8,128)(2,1)} %fusion.16, bf16[128,4,1024]{2,0,1:T(8,128)(2,1)S(1)} %copy-done.1, s32[]{:T(128)S(6)} %select_n.69, s32[]{:T(128)} %constant.22.clone.1, s32[]{:T(128)} %constant.22.clone.1) | dynamic-update-slice | bytes 2097156 | tf_op jit(solution)/shard_map/dynamic_update_slice | solution.py:30
  105.4 23.9 %fusion.7 = bf16[2048,1024]{1,0:T(8,128)(2,1)} fusion(bf16[1,4,1024,2048]{3,2,1,0:T(8,128)(2,1)} %param.7, bf16[1152,4,1024]{2,0,1:T(8,128)(2,1)} %dynamic_update_slice.15), kind=kOutput, calls=%fused_computation.7 | convolution fusion | flops 17181966336 | bytes 29360128 | tf_op jit(solution)/shard_map/prk,lpr->kl/dot_general | solution.py:147
  129.3 0.3 all-gather.2.cloned.1.call-start
  129.5 110.3 %reduce-scatter.2.cloned.1.call-done.cols_ref = bf16[256,1024]{1,0:T(8,128)(2,1)} async-done(((bf16[2048,1024]{1,0:T(8,128)(2,1)}), bf16[256,1024]{1,0:T(8,128)(2,1)}) %reduce-scatter.2.cloned.1.call-update) | async-done | bytes 524304 | tf_op jit(solution)/shard_map/reduce_scatter | solution.py:150
  239.9 0.6 dynamic_slice.47
  241.7 0.7 fusion.17
  242.3 0.7 and_select_fusion.scale_ref
  243.0 72.4 %all-gather.2.cloned.1.call-done = bf16[2048,1024]{1,0:T(8,128)(2,1)} async-done(((bf16[256,1024]{1,0:T(8,128)(2,1)}), bf16[2048,1024]{1,0:T(8,128)(2,1)}) %all-gather.2.cloned.1.call-update) | async-done | bytes 4194320 | tf_op jit(solution)/shard_map/all_gather | solution.py:151
  315.3 7.6 %select_add_fusion.gram_ref = f32[1024,1024]{1,0:T(8,128)S(1)} fusion(f32[1024]{0:T(1024)S(1)} %fusion.17, bf16[2048,1024]{1,0:T(8,128)(2,1)} %all-gather.2.cloned.1.call-done), kind=kOutput, calls=%fused_computation.5 | convolution fusion | flops 4298113024 | bytes 8392704 | tf_op jit(solution)/shard_map/dot_general | solution.py:152
  323.0 76.3 %shard_map.64 = bf16[256,1024]{1,0:T(8,128)(2,1)} custom-call(f32[1024,1024]{1,0:T(8,128)S(1)} %select_add_fusion.gram_ref, bf16[256,1024]{1,0:T(8,128)(2,1)S(1)} %copy-done, f32[1,1024]{1,0:T(1,128)S(1)} %and_select_fusion.scale_ref), custom_call_target="tpu_custom_call" | custom-call | tf_op jit(solution)/shard_map/pallas_call | solution.py:102
  (15 shorter events, 0.4 us)
Async XLA Ops:
  6.5 233.3 %reduce-scatter.2.cloned.1.call-start = ((), (), s32[]{:S(2)}) async-start(), calls=%async_computation.1 | async-start | bytes 4718592 | tf_op jit(solution)/shard_map/reduce_scatter | solution.py:150
  31.3 10.3 %copy-start.2 = (f32[2,4,128]{2,1,0:T(4,128)S(1)}, f32[2,4,128]{2,1,0:T(4,128)}, u32[]{:S(2)}) copy-start(f32[2,4,128]{2,1,0:T(4,128)} %param.10) | copy-start | bytes 12292
  35.5 6.5 %collective-permute-start.1 = (bf16[256,4,1024]{2,0,1:T(8,128)(2,1)}, bf16[256,4,1024]{2,0,1:T(8,128)(2,1)}, u32[]{:S(2)}, u32[]{:S(2)}) collective-permute-start(bf16[256,4,1024]{2,0,1:T(8,128)(2,1)} %pad_maximum_fusion.1), channel_id=1, source_target_pairs={{0,8},{8,16},{16,24},{1,9},{9,17},{17,25},{2,10},{10,18},{18,26},{... | collective-permute-start | bytes 6291464 | tf_op jit(solution)/shard_map/ppermute | solution.py:16
  47.0 27.7 %collective-permute-start = (bf16[256,4,1024]{2,0,1:T(8,128)(2,1)}, bf16[256,4,1024]{2,0,1:T(8,128)(2,1)}, u32[]{:S(2)}, u32[]{:S(2)}) collective-permute-start(bf16[256,4,1024]{2,0,1:T(8,128)(2,1)} %pad_maximum_fusion), channel_id=1, source_target_pairs={{8,0},{16,8},{24,16},{9,1},{17,9},{25,17},{10,2},{18,10},{26,18},{... | collective-permute-start | bytes 6291464 | tf_op jit(solution)/shard_map/ppermute | solution.py:16
  78.5 19.1 %copy-start.1 = (bf16[128,4,1024]{2,0,1:T(8,128)(2,1)S(1)}, bf16[128,4,1024]{2,0,1:T(8,128)(2,1)}, u32[]{:S(2)}) copy-start(bf16[128,4,1024]{2,0,1:T(8,128)(2,1)} %get-tuple-element.5) | copy-start | bytes 3145732
  129.2 110.6 %copy-start.3 = (s32[4]{0:T(128)S(1)}, s32[4]{0:T(128)}, u32[]{:S(2)}) copy-start(s32[4]{0:T(128)} %param.11) | copy-start | bytes 52
  129.3 186.1 %all-gather.2.cloned.1.call-start = ((), (), s32[]{:S(2)}) async-start(), calls=%async_computation.2 | async-start | bytes 4718592 | tf_op jit(solution)/shard_map/all_gather | solution.py:151
  243.0 80.0 %copy-start = (bf16[256,1024]{1,0:T(8,128)(2,1)S(1)}, bf16[256,1024]{1,0:T(8,128)(2,1)}, u32[]{:S(2)}) copy-start(bf16[256,1024]{1,0:T(8,128)(2,1)} %reduce-scatter.2.cloned.1.call-done.cols_ref) | copy-start | bytes 1572868
Sparse Core Ops, SparseCore 0:
  129.4 110.3 reduce-scatter.1
  242.2 73.1 all-gather.1
